TPU v7x, 32 devices: a whole 2x2x4 slice. The times are simulated.
32 devices in a mesh: grp: 4 (over x, core), dev: 8 (over z, y).
Axes of the slice: x: 2, y: 2, z: 4, core: 2. Of those that a mesh axis runs over, the one named last changes fastest.
Arguments:
- samples: bfloat16 [1024, 1024], P(('grp', 'dev')), may hold values from -0.1875 to 0.1875
- set_labels: int32 [1024], P(('grp', 'dev')), may hold values 0 or 1
- sign_words: int32 [1024, 25], P(('grp', 'dev')), may hold values from 0 to 2097151
- corpus: bfloat16 [1024, 1024], P(('grp', 'dev')), may hold values from -0.1875 to 0.1875
- scale_grid: float32 [16], replicated, may hold values from 0.25 to 4
- scale_pick: int32 [4], replicated, may hold values from 0 to 15
Outputs:
- quad_forms: float32 [4, 512], replicated
- test_scores: float32 [4], replicated
- proof: float32 [4, 1024], P(None, ('grp', 'dev'))
Inputs may be any that keep to these rules, and one draw needn't show every extreme that they name: `sign_words`: every word is below 2 ** 21; each of its 21 bits is a sign, 1 for +1 and 0 for -1. `scale_pick`: indices into the grid, from 0 to 15.
All inputs are finite; a program needn't handle non-finite values. No bound on the sum of `set_labels` on one device may be relied on, other than what follows from the above.
Results may differ from a plain program's by a relative error of at most 0.0099.
Values may be sent and summed in bfloat16 or wider, within the bound.
A program may use at most 64 MiB of HBM per device.

v0:
```python
import jax
import jax.numpy as jnp
from jax import lax
from jax.sharding import PartitionSpec as P

NB = 4
BOOT = 511


word_bits = 21


def make_vectors(set_labels, sign_words):
    weights = (1 - 2 * set_labels).astype(jnp.float32)
    shifts = jnp.arange(word_bits, dtype=jnp.int32)
    bit_flags = jnp.right_shift(sign_words[:, :, None], shifts[None, None, :]) & 1
    bit_flags = bit_flags.reshape(sign_words.shape[0], -1)[:, :BOOT]
    sign_values = (2 * bit_flags - 1).astype(jnp.float32)
    vectors = jnp.concatenate([weights[:, None], sign_values * weights[:, None]], axis=1)
    return vectors.astype(jnp.bfloat16)


def band_scales(scale_grid, scale_pick):
    onehot = (
        scale_pick[:, None] == jnp.arange(scale_grid.shape[0], dtype=jnp.int32)[None, :]
    ).astype(jnp.float32)
    chosen = jnp.sum(onehot * scale_grid[None, :], axis=1)
    return 0.5 / chosen


def squares(matrix):
    wide = matrix.astype(jnp.float32)
    return jnp.sum(wide * wide, axis=1)


def distances(left, left_sq, right, right_sq):
    cross = lax.dot_general(
        left, right, (((1,), (1,)), ((), ())), preferred_element_type=jnp.float32
    )
    return left_sq[:, None] + right_sq[None, :] - 2.0 * cross


def test_terms(block_rows, block_vec, col_rows, col_sq, col_vec, scales):
    dist = distances(block_rows, squares(block_rows), col_rows, col_sq)
    block_wide = block_vec.astype(jnp.float32)
    results = []
    for kernel_id in range(NB):
        kern = jnp.exp(-dist * scales[kernel_id]).astype(jnp.bfloat16)
        product = jnp.dot(kern, col_vec, preferred_element_type=jnp.float32)
        results.append(jnp.sum(block_wide * product, axis=0))
    return jnp.stack(results)


def proof_terms(corp_rows, corp_sq, sample_rows, sample_sq, sample_weights, scales):
    dist = distances(corp_rows, corp_sq, sample_rows, sample_sq)
    results = []
    for kernel_id in range(NB):
        kern = jnp.exp(-dist * scales[kernel_id]).astype(jnp.bfloat16)
        results.append(jnp.dot(kern, sample_weights, preferred_element_type=jnp.float32))
    return jnp.stack(results)


def per_device(samples, set_labels, sign_words, corpus, scale_grid, scale_pick):
    scales = band_scales(scale_grid, scale_pick)
    col_rows, col_labels, col_words = (
        lax.all_gather(samples, "grp", axis=0, tiled=True),
        lax.all_gather(set_labels, "grp", axis=0, tiled=True),
        lax.all_gather(sign_words, "grp", axis=0, tiled=True),
    )
    col_vec = make_vectors(col_labels, col_words)
    col_sq = squares(col_rows)
    total = col_rows.shape[0] * lax.axis_size("dev")
    inv_root = jnp.float32(1.0) / jnp.sqrt(jnp.float32(total))
    block_rows = lax.all_gather(samples, "dev", axis=0, tiled=True)
    block_labels = lax.all_gather(set_labels, "dev", axis=0, tiled=True)
    block_words = lax.all_gather(sign_words, "dev", axis=0, tiled=True)
    block_vec = make_vectors(block_labels, block_words)
    forms_part = test_terms(block_rows, block_vec, col_rows, col_sq, col_vec, scales)
    group_corpus = lax.all_gather(corpus, "dev", axis=0, tiled=True)
    proof_part = proof_terms(
        group_corpus, squares(group_corpus), col_rows, col_sq, col_vec[:, 0], scales
    )
    proof = lax.psum_scatter(proof_part, "dev", scatter_dimension=1, tiled=True) * inv_root
    quad_forms = lax.psum(forms_part, ("grp", "dev")) / total
    bootstrap = quad_forms[:, 1:]
    centre = jnp.mean(bootstrap, axis=1)
    spread = jnp.mean(jnp.square(bootstrap - centre[:, None]), axis=1)
    test_scores = (quad_forms[:, 0] - centre) / jnp.sqrt(spread + 1e-06)
    return (quad_forms, test_scores, proof)


def solution(mesh):
    in_specs = (
        P(("grp", "dev"), None),
        P(("grp", "dev")),
        P(("grp", "dev"), None),
        P(("grp", "dev"), None),
        P(),
        P(),
    )
    out_specs = (P(), P(), P(None, ("grp", "dev")))
    return jax.shard_map(
        per_device, mesh=mesh, in_specs=in_specs, out_specs=out_specs, check_vma=False
    )
```

profile of v0, /device:TPU:0, one launch (start us, length us, event | category | flops | bytes accessed | tf_op | source)
XLA Modules:
  0.0 194.1 jit_solution(99194032742411374)
XLA Ops:
  7.2 0.0 reduce-scatter.4.cloned.1.call-start
  7.2 0.0 copy-start.4
  7.2 0.0 copy-start.5
  7.2 0.6 copy-done.4
  7.9 0.0 copy-done.5
  7.9 0.2 select_reduce_fusion
  8.1 0.0 copy-start.8
  8.1 0.6 copy-done.8
  8.7 0.6 dynamic-slice.1
  10.0 0.0 copy-start.6
  10.0 0.6 copy-done.6
  10.6 0.2 dynamic-update-slice.1
  10.8 6.3 %all-reduce.1 = s32[128]{0:T(128)S(1)} all-reduce(s32[128]{0:T(128)S(1)} %dynamic-update-slice.1), channel_id=1, replica_groups=mesh['grp'=4,'dev'=8] {'grp'}, use_global_device_ids=true, to_apply=%add.1 | all-reduce | flops 128 | bytes 1024
  17.2 0.7 fusion.33
  17.8 6.0 %all_gather.24 = bf16[128,1024]{1,0:T(8,128)(2,1)S(1)} all-gather(bf16[32,1024]{1,0:T(8,128)(2,1)} %param.6), channel_id=1, replica_groups=mesh['grp'=4,'dev'=8] {'grp'}, dimensions={0}, use_global_device_ids=true | all-gather | bytes 327680 | tf_op jit(solution)/shard_map/all_gather | solution.py:66
  23.8 0.0 copy-start.2
  23.8 0.1 multiply_reduce_fusion.2
  23.9 0.7 copy-done.2
  24.6 31.9 %all_gather.27 = bf16[256,1024]{1,0:T(8,128)(2,1)S(1)} all-gather(bf16[32,1024]{1,0:T(8,128)(2,1)S(1)} %copy-done.2), channel_id=1, replica_groups=mesh['grp'=4,'dev'=8] {'dev'}, dimensions={0}, use_global_device_ids=true | all-gather | bytes 589824 | tf_op jit(solution)/shard_map/all_gather | solution.py:79
  56.5 0.2 multiply_reduce_fusion
  56.7 0.3 fusion.5
  57.0 0.8 fusion.23
  57.8 0.8 fusion.22
  58.6 0.8 fusion.21
  59.5 0.8 fusion.20
  60.3 0.8 copy.32
  61.1 0.0 copy-start.3
  61.1 0.0 reduce-scatter.4.cloned.1.call-update
  61.1 0.7 copy-done.3
  61.8 5.2 %all_gather.26 = s32[128,25]{1,0:T(8,128)S(1)} all-gather(s32[32,25]{1,0:T(8,128)S(1)} %copy-done.3), channel_id=1, replica_groups=mesh['grp'=4,'dev'=8] {'grp'}, dimensions={0}, use_global_device_ids=true | all-gather | bytes 16000 | tf_op jit(solution)/shard_map/all_gather | solution.py:68
  67.0 0.0 copy-start
  67.0 30.6 %all_gather.22 = s32[256,25]{1,0:T(8,128)S(1)} all-gather(s32[32,25]{1,0:T(8,128)S(1)} %copy-done.3), channel_id=1, replica_groups=mesh['grp'=4,'dev'=8] {'dev'}, dimensions={0}, use_global_device_ids=true | all-gather | bytes 28800 | tf_op jit(solution)/shard_map/all_gather | solution.py:76
  97.7 0.0 copy-done
  97.7 0.0 copy-start.7
  97.7 31.5 %all_gather.23 = bf16[256,1024]{1,0:T(8,128)(2,1)S(1)} all-gather(bf16[32,1024]{1,0:T(8,128)(2,1)S(1)} %copy-done), channel_id=1, replica_groups=mesh['grp'=4,'dev'=8] {'dev'}, dimensions={0}, use_global_device_ids=true | all-gather | bytes 589824 | tf_op jit(solution)/shard_map/all_gather | solution.py:74
  129.1 0.0 copy-done.7
  129.1 0.6 dynamic-slice
  130.4 0.2 dynamic-update-slice
  130.7 10.8 %all-reduce = s32[256]{0:T(256)S(1)} all-reduce(s32[256]{0:T(256)S(1)} %dynamic-update-slice), channel_id=1, replica_groups=mesh['grp'=4,'dev'=8] {'dev'}, use_global_device_ids=true, to_apply=%add | all-reduce | flops 256 | bytes 2048
  141.5 0.1 shift_right_arithmetic.43
  141.6 0.1 copy.23
  141.6 0.1 copy.22
  141.8 0.2 multiply_reduce_fusion.1
  142.0 0.3 fusion.7
  142.4 0.1 shift_right_arithmetic.41
  142.4 0.1 fusion.19
  142.6 0.2 fusion.13
  142.8 1.0 fusion.3
  143.8 1.0 fusion.2
  144.8 1.0 fusion.1
  145.8 1.0 fusion
  146.9 37.9 %psum.7 = f32[4,512]{1,0:T(4,128)S(1)} all-reduce(f32[4,512]{1,0:T(4,128)S(1)} %pad_maximum_fusion.2), channel_id=1, replica_groups=mesh['grp'=4,'dev'=8] {'grp','dev'}, use_global_device_ids=true, to_apply=%region_7.0 | all-reduce | flops 2048 | bytes 16384 | tf_op jit(solution)/shard_map/psum | solution.py:84
  184.7 0.0 copy-start.1
  184.7 0.2 slice_reduce_fusion
  184.9 0.1 slice_reduce_fusion.1
  185.0 0.2 multiply_reduce_fusion.3
  185.2 0.1 copy-done.1
  185.3 0.5 rsqrt_multiply_fusion
  185.9 0.0 reduce-scatter.4.cloned.1.call-done
  185.9 0.8 copy.33
  186.6 0.6 broadcast_multiply_fusion.1
  (15 shorter events, 0.2 us)
Async XLA Ops:
  7.2 178.7 %reduce-scatter.4.cloned.1.call-start = ((), (), s32[]{:S(2)}) async-start(), calls=%async_computation.1 | async-start | bytes 147456
  7.2 0.7 copy-start.4
  7.2 0.7 copy-start.5
  8.1 0.7 copy-start.8
  10.0 0.7 copy-start.6
  23.8 0.8 copy-start.2
  61.1 0.7 copy-start.3
  67.0 30.6 %copy-start = (bf16[32,1024]{1,0:T(8,128)(2,1)S(1)}, bf16[32,1024]{1,0:T(8,128)(2,1)}, u32[]{:S(2)}) copy-start(bf16[32,1024]{1,0:T(8,128)(2,1)} %param.6) | copy-start | bytes 196612
  97.7 31.5 %copy-start.7 = (u32[32]{0:T(128)S(1)}, u32[32]{0:T(128)}, u32[]{:S(2)}) copy-start(u32[32]{0:T(128)} %constant.35) | copy-start | bytes 388
  184.7 0.6 copy-start.1
Sparse Core Ops, SparseCore 0:
  61.2 61.4 reduce-scatter.3
where the time goes:
time: 195 us; the launch traced here: 194 us
  blocking collectives  160 us (82%)
  between operations  15.5 us (8%)
  matrix products  7.93 us (4%)
  local copies, waits for them, and re-layouts  7.86 us (4%)
  other arithmetic  2.55 us (1%)
    psum x1, blocking collectives, per_device(): quad_forms = lax.psum(forms_part, ('grp', 'dev')) / total  37.9 us
    all_gather x1, blocking collectives, per_device(): group_corpus = lax.all_gather(corpus, 'dev', axis=0, tiled=True)  31.9 us
    all_gather x1, blocking collectives, per_device(): block_rows = lax.all_gather(samples, 'dev', axis=0, tiled=True)  31.5 us
    all_gather x1, blocking collectives, per_device(): block_words = lax.all_gather(sign_words, 'dev', axis=0, tiled=True)  30.6 us
    unnamed x2, blocking collectives  17.1 us
    unnamed x26, local copies, waits for them, and re-layouts  6.66 us
    all_gather x1, blocking collectives, per_device(): lax.all_gather(samples, 'grp', axis=0, tiled=True)  5.98 us
    all_gather x1, blocking collectives, per_device(): lax.all_gather(sign_words, 'grp', axis=0, tiled=True)  5.23 us
  transfers between devices with their start and end apart: 1, of which 0 were waited for; matrix products, arithmetic and copies ran while one was open for 4% of the time, Pallas kernels for 0%

commit v1 on v0

v1 whole, which is shorter than its diff:
```python
import functools
import math

import jax
import jax.numpy as jnp
from jax import lax
from jax.experimental import pallas as pl
from jax.experimental.pallas import tpu as pltpu
from jax.sharding import PartitionSpec as P

WORD_BITS = 21
CORES = 2
LOG2E = math.log2(math.e)
MESH = pl.DeviceIdType.MESH
F32 = jnp.float32
BF16 = jnp.bfloat16


def loop(count, body):
    if count == 1:
        body(0)
    else:
        lax.fori_loop(0, count, lambda i, c: (body(i), c)[1], 0)


def aligned(index, size):
    return index * size if isinstance(index, int) else pl.multiple_of(index * size, size)


def kernel(geo, samples, labels, words, corpus, grid, pick, quad_out, score_out, proof_out,
           row_s, row_c, col_s, word_in, label_in, row_pack, col_pack, row_vec, col_vec,
           part1, part2, local_sem, rp_send, rp_recv, cp_send, cp_recv, rs_send, rs_recv,
           rc_send, rc_recv, cs_send, cs_recv, fw_send, fw_recv, p1_send, p1_recv, p2_send, p2_recv):
    n_gx, n_lo, n_hi = geo
    own = samples.shape[0]
    n_bands, n_vec = quad_out.shape
    n_row, n_col, n_plane = n_gx * n_lo, n_hi * CORES, n_gx * n_lo * CORES
    rows, cols = n_row * own, n_col * own
    n_words = words.shape[1]
    total = n_row * n_col * own

    grp, dev = lax.axis_index("grp"), lax.axis_index("dev")
    gx, core = grp // CORES, grp % CORES
    z, lo = dev // n_lo, dev % n_lo
    other = 1 - core
    rslot = gx * n_lo + lo
    cslot = z * CORES + core
    pslot = rslot * CORES + core

    def at_row(slot, core_):
        return ((slot // n_lo) * CORES + core_, z * n_lo + slot % n_lo)

    def at_col(z_, core_):
        return (gx * CORES + core_, z_ * n_lo + lo)

    barrier = pltpu.get_barrier_semaphore()
    partners = []
    for t in range(1, n_plane):
        slot = (pslot + t) % n_plane
        partners.append(at_row(slot // CORES, slot % CORES))
    for t in range(1, n_hi):
        partners.append(at_col((z + t) % n_hi, core))
        partners.append(at_col((z + t) % n_hi, other))

    word_copy = pltpu.make_async_copy(words, word_in, local_sem.at[0])
    label_copy = pltpu.make_async_copy(labels, label_in, local_sem.at[1])
    word_copy.start()
    label_copy.start()
    for p in partners:
        pl.semaphore_signal(barrier, inc=1, device_id=p, device_id_type=MESH)
    own_rows = pl.ds(pl.multiple_of(rslot * own, own), own)
    own_cols = pl.ds(pl.multiple_of(cslot * own, own), own)
    keep = [
        pltpu.make_async_copy(samples, row_s.at[own_rows], local_sem.at[2]),
        pltpu.make_async_copy(corpus, row_c.at[own_rows], local_sem.at[3]),
        pltpu.make_async_copy(samples, col_s.at[own_cols], local_sem.at[4]),
    ]
    for c in keep:
        c.start()

    pl.semaphore_wait(barrier, len(partners))

    def remote(src, dst, send, recv, to):
        return pltpu.make_async_remote_copy(
            src_ref=src, dst_ref=dst, send_sem=send, recv_sem=recv, device_id=to, device_id_type=MESH)

    sends = []
    col_in, fw_in, rs_in, rc_in = [], [], [], []

    def col_block(slot):
        return col_s.at[pl.ds(pl.multiple_of(slot * own, own), own)]

    def row_block(ref, slot):
        return ref.at[pl.ds(pl.multiple_of(slot * own, own), own)]

    for t in range(1, n_hi):
        to = (z + t) % n_hi
        c = remote(samples, col_block(cslot), cs_send.at[t], cs_recv.at[z], at_col(to, core))
        c.start()
        sends.append(c)
    for t in range(1, n_row):
        to = (rslot + t) % n_row
        c = remote(samples, row_block(row_s, rslot), rs_send.at[t], rs_recv.at[rslot], at_row(to, core))
        c.start()
        sends.append(c)
    c = remote(samples, col_block(cslot), fw_send.at[z], fw_recv.at[z], at_col(z, other))
    c.start()
    sends.append(c)

    word_copy.wait()
    label_copy.wait()
    eye = lax.broadcasted_iota(jnp.int32, (own, own), 0) == lax.broadcasted_iota(jnp.int32, (own, own), 1)
    label_col = jnp.sum(jnp.where(eye, label_in[...].astype(F32), 0.0), axis=1, keepdims=True).astype(jnp.int32)
    groups = own // 8
    pieces = []
    width = 128 // groups
    for q in range(groups):
        pieces.append(word_in[pl.ds(8 * q, 8), :])
        pieces.append(label_col[8 * q:8 * q + 8])
        pieces.append(jnp.zeros((8, width - n_words - 1), jnp.int32))
    packed = jnp.concatenate(pieces, axis=1)
    col_pack[cslot] = packed
    row_pack[rslot] = packed

    for t in range(1, n_col):
        to = (cslot + t) % n_col
        c = remote(col_pack.at[cslot], col_pack.at[cslot], cp_send.at[t], cp_recv.at[cslot],
                   at_col(to // CORES, to % CORES))
        c.start()
        sends.append(c)
    for t in range(1, n_row):
        to = (rslot + t) % n_row
        c = remote(row_pack.at[rslot], row_pack.at[rslot], rp_send.at[t], rp_recv.at[rslot], at_row(to, core))
        c.start()
        sends.append(c)
    for t in range(1, n_row):
        to = (rslot + t) % n_row
        c = remote(corpus, row_block(row_c, rslot), rc_send.at[t], rc_recv.at[rslot], at_row(to, core))
        c.start()
        sends.append(c)

    for t in range(1, n_hi):
        src = (z + n_hi - t) % n_hi
        block = col_block(src * CORES + core)
        remote(samples, block, cs_send.at[t], cs_recv.at[src], at_col(src, core)).wait_recv()
        c = remote(block, block, fw_send.at[src], fw_recv.at[src], at_col(z, other))
        c.start()
        sends.append(c)

    lane = lax.broadcasted_iota(jnp.int32, (8, 128), 1)
    label_lane = lane - lane % width + n_words
    is_label = lane % width == n_words
    n_chunks = n_vec // 128
    index, mask = [], []
    for t in range(n_chunks):
        k = jnp.maximum(lane + (128 * t - 1), 0)
        w = (k * 3121) >> 16
        shift = k - w * WORD_BITS
        if t == 0:
            w = jnp.where(lane == 0, n_words, w)
            shift = jnp.where(lane == 0, 0, shift)
        index.append(w)
        mask.append(jnp.int32(1) << shift)

    def expand(tile, dst, base):
        label = jnp.take_along_axis(tile, label_lane, axis=1)
        tile = jnp.where(is_label, label ^ 1, tile ^ (0 - label))
        for t in range(n_chunks):
            parts = []
            for q in range(groups):
                got = jnp.take_along_axis(tile, index[t] + q * width, axis=1)
                parts.append(jnp.where((got & mask[t]) != 0, 1.0, -1.0).astype(F32))
            dst[pl.ds(base, own), pl.ds(128 * t, 128)] = jnp.concatenate(parts, axis=0).astype(dst.dtype)

    for t in range(1, n_col):
        src = (cslot + n_col - t) % n_col
        remote(col_pack.at[src], col_pack.at[src], cp_send.at[t], cp_recv.at[src],
               at_col(src // CORES, src % CORES)).wait_recv()
    for t in range(1, n_row):
        src = (rslot + n_row - t) % n_row
        remote(row_pack.at[src], row_pack.at[src], rp_send.at[t], rp_recv.at[src], at_row(src, core)).wait_recv()
    for slot in range(n_col):
        expand(col_pack[slot], col_vec, slot * own)
    for slot in range(n_row):
        expand(row_pack[slot], row_vec, slot * own)

    for c in keep:
        c.wait()
    for t in range(n_hi):
        src = (z + n_hi - t) % n_hi
        block = col_block(src * CORES + other)
        remote(samples, block, fw_send.at[src], fw_recv.at[src], at_col(z, other)).wait_recv()
    for t in range(1, n_row):
        src = (rslot + n_row - t) % n_row
        remote(samples, row_block(row_s, src), rs_send.at[t], rs_recv.at[src], at_row(src, core)).wait_recv()
    for t in range(1, n_row):
        src = (rslot + n_row - t) % n_row
        remote(corpus, row_block(row_c, src), rc_send.at[t], rc_recv.at[src], at_row(src, core)).wait_recv()

    rb, cb = min(128, rows), min(256, cols)
    gains = [jnp.full((1, 1), -0.5 * LOG2E, F32) / jnp.full((1, 1), grid[pick[b]], F32) for b in range(n_bands)]
    diag = lax.broadcasted_iota(jnp.int32, (cb, cb), 0) == lax.broadcasted_iota(jnp.int32, (cb, cb), 1)
    if rows > rb or cols > cb:
        part1[pslot] = jnp.zeros(part1.shape[1:], F32)

    def squares(x):
        wide = x.astype(F32)
        return jnp.sum(wide * wide, axis=1, keepdims=True)

    def kerns(left, right, right_sq):
        cross = lax.dot_general(left, right, (((1,), (1,)), ((), ())), preferred_element_type=F32)
        dist = squares(left) + right_sq - 2.0 * cross
        return jnp.concatenate([jnp.exp2(dist * g).astype(BF16) for g in gains], axis=0)

    def add_to(lanes, value):
        if rows > rb or cols > cb:
            value = part1[pslot, :, lanes] + value
        part1[pslot, :, lanes] = value

    def column_chunk(cc):
        here = pl.ds(aligned(cc, cb), cb)
        right = col_s[here, :]
        right_sq = jnp.sum(jnp.where(diag, squares(right), 0.0), axis=0, keepdims=True)
        vec = col_vec[here, :]

        def row_chunk(rc):
            there = pl.ds(aligned(rc, rb), rb)
            kern = kerns(row_s[there, :], right, right_sq)
            prod = jnp.dot(kern, vec, preferred_element_type=F32)
            mine = row_vec[there, :]
            forms = [jnp.sum(mine * prod[b * rb:(b + 1) * rb], axis=0, keepdims=True) for b in range(n_bands)]
            add_to(pl.ds(0, n_vec), jnp.concatenate(forms, axis=0))
            kern = kerns(row_c[there, :], right, right_sq)
            flat = lax.dot_general(vec[:, :128], kern, (((0,), (1,)), ((), ())), preferred_element_type=F32)
            proof = jnp.concatenate([flat[0:1, b * rb:(b + 1) * rb] for b in range(n_bands)], axis=0)
            add_to(pl.ds(aligned(rc, rb) + n_vec, rb), proof)

        loop(rows // rb, row_chunk)

    loop(cols // cb, column_chunk)

    for t in range(1, n_plane):
        to = (pslot + t) % n_plane
        c = remote(part1.at[pslot], part1.at[pslot], p1_send.at[t], p1_recv.at[pslot],
                   at_row(to // CORES, to % CORES))
        c.start()
        sends.append(c)
    for t in range(1, n_plane):
        src = (pslot + n_plane - t) % n_plane
        remote(part1.at[src], part1.at[src], p1_send.at[t], p1_recv.at[src],
               at_row(src // CORES, src % CORES)).wait_recv()
    quad = part1[0, :, :n_vec]
    for slot in range(1, n_plane):
        quad = quad + part1[slot, :, :n_vec]
    part2[z] = quad
    for t in range(1, n_hi):
        to = (z + t) % n_hi
        c = remote(part2.at[z], part2.at[z], p2_send.at[t], p2_recv.at[z], at_col(to, core))
        c.start()
        sends.append(c)
    proof = part1[core, :, n_vec:]
    for slot in range(1, n_row):
        proof = proof + part1[slot * CORES + core, :, n_vec:]
    mine = jnp.zeros((n_bands, own), F32)
    for slot in range(n_row):
        mine = jnp.where(rslot == slot, proof[:, slot * own:(slot + 1) * own], mine)
    proof_out[...] = mine * F32(1.0 / math.sqrt(total))
    for t in range(1, n_hi):
        src = (z + n_hi - t) % n_hi
        remote(part2.at[src], part2.at[src], p2_send.at[t], p2_recv.at[src], at_col(src, core)).wait_recv()
    quad = part2[0]
    for slot in range(1, n_hi):
        quad = quad + part2[slot]
    quad = quad * F32(1.0 / total)
    quad_out[...] = quad
    boot = lax.broadcasted_iota(jnp.int32, quad.shape, 1) > 0
    count = F32(1.0 / (n_vec - 1))
    centre = jnp.sum(jnp.where(boot, quad, 0.0), axis=1, keepdims=True) * count
    off = quad - centre
    spread = jnp.sum(jnp.where(boot, off * off, 0.0), axis=1, keepdims=True) * count
    score = (quad[:, :1] - centre) / jnp.sqrt(spread + 1e-6)
    spot = lax.broadcasted_iota(jnp.int32, (n_bands, n_bands), 0) == lax.broadcasted_iota(
        jnp.int32, (n_bands, n_bands), 1)
    score_out[...] = jnp.sum(jnp.where(spot, score, 0.0), axis=0, keepdims=True)
    for c in sends:
        c.wait_send()


def per_device(n_grp, n_dev, samples, labels, words, corpus, grid, pick):
    n_lo = 2 if n_dev % 2 == 0 else 1
    n_gx, n_hi = n_grp // CORES, n_dev // n_lo
    n_row, n_col, n_plane = n_gx * n_lo, n_hi * CORES, n_gx * n_lo * CORES
    own, width = samples.shape
    rows, cols = n_row * own, n_col * own
    n_bands, n_vec = pick.shape[0], 512
    dma = lambda n: pltpu.SemaphoreType.DMA((n,))
    any_ = pl.BlockSpec(memory_space=pl.ANY)
    vmem = pl.BlockSpec(memory_space=pltpu.VMEM)
    smem = pl.BlockSpec(memory_space=pltpu.SMEM)
    quad, score, proof = pl.pallas_call(
        functools.partial(kernel, (n_gx, n_lo, n_hi)),
        out_shape=(
            jax.ShapeDtypeStruct((n_bands, n_vec), F32),
            jax.ShapeDtypeStruct((1, n_bands), F32),
            jax.ShapeDtypeStruct((n_bands, own), F32),
        ),
        in_specs=[any_, any_, any_, any_, smem, smem],
        out_specs=(vmem, vmem, vmem),
        scratch_shapes=[
            pltpu.VMEM((rows, width), BF16),
            pltpu.VMEM((rows, width), BF16),
            pltpu.VMEM((cols, width), BF16),
            pltpu.VMEM(words.shape, jnp.int32),
            pltpu.VMEM((1, own), jnp.int32),
            pltpu.VMEM((n_row, 8, 128), jnp.int32),
            pltpu.VMEM((n_col, 8, 128), jnp.int32),
            pltpu.VMEM((rows, n_vec), F32),
            pltpu.VMEM((cols, n_vec), BF16),
            pltpu.VMEM((n_plane, n_bands, n_vec + rows), F32),
            pltpu.VMEM((n_hi, n_bands, n_vec), F32),
            dma(5),
            dma(n_row), dma(n_row), dma(n_col), dma(n_col), dma(n_row), dma(n_row),
            dma(n_row), dma(n_row), dma(n_hi), dma(n_hi), dma(n_hi), dma(n_hi),
            dma(n_plane), dma(n_plane), dma(n_hi), dma(n_hi),
        ],
        compiler_params=pltpu.CompilerParams(
            collective_id=0, has_side_effects=True, vmem_limit_bytes=48 * 1024 * 1024),
        name="two_sample",
    )(samples, labels.reshape(1, own), words, corpus, grid, pick)
    return quad, score.reshape(n_bands), proof


def solution(mesh):
    in_specs = (
        P(("grp", "dev"), None),
        P(("grp", "dev")),
        P(("grp", "dev"), None),
        P(("grp", "dev"), None),
        P(),
        P(),
    )
    out_specs = (P(), P(), P(None, ("grp", "dev")))
    return jax.shard_map(
        functools.partial(per_device, mesh.shape["grp"], mesh.shape["dev"]),
        mesh=mesh, in_specs=in_specs, out_specs=out_specs, check_vma=False
    )
```

time: 195 us -> 30.9 us (0.16)
  blocking collectives: 160 us -> 0 us
  Pallas kernels: 0 us -> 25.2 us
  between operations: 15.5 us -> 0.67 us
  matrix products: 7.93 us -> 0 us
  local copies, waits for them, and re-layouts: 7.86 us -> 4.75 us
  other arithmetic: 2.55 us -> 0 us
    all_gather x5 -> x0, blocking collectives: 105 us -> none  [the longest x1 31.9 us: per_device(): group_corpus = lax.all_gather(corpus, 'dev', axis=0, tiled=True)]
    psum x1 -> x0, blocking collectives: 37.9 us -> none  [per_device(): quad_forms = lax.psum(forms_part, ('grp', 'dev')) / total]
    pallas_call x0 -> x1, Pallas kernels: none -> 25.2 us  [per_device(): pl.pallas_call(functools.partial(kernel, (n_gx, n_lo, n_hi)), out_shape=(...]
    unnamed x2 -> x0, blocking collectives: 17.1 us -> none
    dot_general x10 -> x0, matrix products: 7.93 us -> none  [the longest x4 4.08 us: test_terms(): product = jnp.dot(kern, col_vec, preferred_element_type=jnp.float32)]
    unnamed x26 -> x15, local copies, waits for them, and re-layouts: 6.66 us -> 4.75 us
  transfers between devices with their start and end apart: 1 -> 0, of which waited for: 0 -> 0; matrix products, arithmetic and copies ran while one was open for 4% -> 0% of each run, Pallas kernels for 0% -> 0%
where the time goes in v1:
time: 30.9 us; the launch traced here: 30.6 us
  Pallas kernels  25.2 us (82%)
  local copies, waits for them, and re-layouts  4.75 us (15%)
  between operations  0.67 us (2%)
    pallas_call x1, Pallas kernels, per_device(): pl.pallas_call(functools.partial(kernel, (n_gx, n_lo, n_hi)), out_shape=(...  25.2 us
    unnamed x15, local copies, waits for them, and re-layouts  4.75 us

profile of v1, /device:TPU:0, one launch (start us, length us, event | category | flops | bytes accessed | tf_op | source)
XLA Modules:
  0.0 30.6 jit_solution(14901755759140391319)
XLA Ops:
  0.6 0.0 copy-start.5
  0.6 0.0 copy-start.4
  0.7 0.0 copy-start.3
  0.7 0.6 %copy-done.5 = s32[4]{0:T(128)S(1)} copy-done((s32[4]{0:T(128)S(1)}, s32[4]{0:T(128)}, u32[]{:S(2)}) %copy-start.5) | copy-done | bytes 40
  1.3 0.0 copy-done.4
  1.3 0.0 copy-done.3
  1.3 0.0 copy-start
  1.3 0.8 %copy-done = bf16[32,1024]{1,0:T(8,128)(2,1)S(1)} copy-done((bf16[32,1024]{1,0:T(8,128)(2,1)S(1)}, bf16[32,1024]{1,0:T(8,128)(2,1)}, u32[]{:S(2)}) %copy-start) | copy-done | bytes 65560
  2.2 0.0 copy-start.1
  2.2 0.8 %copy-done.1 = bf16[32,1024]{1,0:T(8,128)(2,1)S(1)} copy-done((bf16[32,1024]{1,0:T(8,128)(2,1)S(1)}, bf16[32,1024]{1,0:T(8,128)(2,1)}, u32[]{:S(2)}) %copy-start.1) | copy-done | bytes 65560
  3.0 0.0 copy-start.2
  3.0 0.7 %copy-done.2 = s32[32,25]{1,0:T(8,128)S(1)} copy-done((s32[32,25]{1,0:T(8,128)S(1)}, s32[32,25]{1,0:T(8,128)}, u32[]{:S(2)}) %copy-start.2) | copy-done | bytes 3224
  3.7 25.2 %two_sample.1 = (f32[4,512]{1,0:T(4,128)S(1)}, f32[1,4]{1,0:T(1,128)S(1)}, f32[4,32]{1,0:T(4,128)S(1)}) custom-call(bf16[32,1024]{1,0:T(8,128)(2,1)S(1)} %copy-done, s32[1,32]{1,0:T(1,128)S(1)} %bitcast.2, s32[32,25]{1,0:T(8,128)S(1)} %copy-done.2, bf16[32,1024]{1,0:T(8,128)(2,1)S(1)} %copy-done.1, f32[16]{0:T(128)S(1)} %copy-done.4, s32[4]{0:T(128)S(1)} %copy-done.5), custom_call_target="tpu_custom_call" | custom-call | tf_op jit(solution)/shard_map/two_sample/pallas_call | solution.py:300
  28.9 0.6 %copy.12 = f32[4,512]{1,0:T(4,128)} copy(f32[4,512]{1,0:T(4,128)S(1)} %get-tuple-element.12) | data formatting | bytes 16384
  29.5 0.5 %copy.13 = f32[4]{0:T(128)} copy(f32[4]{0:T(128)S(1)} %bitcast.3) | data formatting | bytes 32
  30.0 0.6 %copy.14 = f32[4,32]{1,0:T(4,128)} copy(f32[4,32]{1,0:T(4,128)S(1)} %get-tuple-element.14) | data formatting | bytes 1024
Async XLA Ops:
  0.6 0.7 %copy-start.5 = (s32[4]{0:T(128)S(1)}, s32[4]{0:T(128)}, u32[]{:S(2)}) copy-start(s32[4]{0:T(128)} %pick.1) | copy-start | bytes 52
  0.6 0.7 %copy-start.4 = (f32[16]{0:T(128)S(1)}, f32[16]{0:T(128)}, u32[]{:S(2)}) copy-start(f32[16]{0:T(128)} %grid.1) | copy-start | bytes 196
  0.7 0.7 %copy-start.3 = (s32[32]{0:T(128)S(1)}, s32[32]{0:T(128)}, u32[]{:S(2)}) copy-start(s32[32]{0:T(128)} %param.7) | copy-start | bytes 388
  1.3 0.8 %copy-start = (bf16[32,1024]{1,0:T(8,128)(2,1)S(1)}, bf16[32,1024]{1,0:T(8,128)(2,1)}, u32[]{:S(2)}) copy-start(bf16[32,1024]{1,0:T(8,128)(2,1)} %samples.1) | copy-start | bytes 196612
  2.2 0.8 %copy-start.1 = (bf16[32,1024]{1,0:T(8,128)(2,1)S(1)}, bf16[32,1024]{1,0:T(8,128)(2,1)}, u32[]{:S(2)}) copy-start(bf16[32,1024]{1,0:T(8,128)(2,1)} %corpus.1) | copy-start | bytes 196612
  3.0 0.7 %copy-start.2 = (s32[32,25]{1,0:T(8,128)S(1)}, s32[32,25]{1,0:T(8,128)}, u32[]{:S(2)}) copy-start(s32[32,25]{1,0:T(8,128)} %words.1) | copy-start | bytes 9604

commit v2 on v1

--- a/solution.py
+++ b/solution.py
@@ -28,9 +28,10 @@
 
 
 def kernel(geo, samples, labels, words, corpus, grid, pick, quad_out, score_out, proof_out,
-           row_s, row_c, col_s, word_in, label_in, row_pack, col_pack, row_vec, col_vec,
-           part1, part2, local_sem, rp_send, rp_recv, cp_send, cp_recv, rs_send, rs_recv,
-           rc_send, rc_recv, cs_send, cs_recv, fw_send, fw_recv, p1_send, p1_recv, p2_send, p2_recv):
+           row_s, row_c, col_s, word_in, label_in, grid_in, pick_in, row_pack, col_pack, row_vec, col_vec,
+           part1, part2, pair_sem, local_sem, rp_send, rp_recv, rs_send, rs_recv, rc_send, rc_recv,
+           cp_send, cp_recv, cs_send, cs_recv, fp_send, fp_recv, fw_send, fw_recv,
+           p1_send, p1_recv, p2_send, p2_recv):
     n_gx, n_lo, n_hi = geo
     own = samples.shape[0]
     n_bands, n_vec = quad_out.shape
@@ -54,58 +55,52 @@
         return (gx * CORES + core_, z_ * n_lo + lo)
 
     barrier = pltpu.get_barrier_semaphore()
-    partners = []
-    for t in range(1, n_plane):
-        slot = (pslot + t) % n_plane
-        partners.append(at_row(slot // CORES, slot % CORES))
-    for t in range(1, n_hi):
-        partners.append(at_col((z + t) % n_hi, core))
-        partners.append(at_col((z + t) % n_hi, other))
+    up, down = z < n_hi - 1, z > 0
+    partners = [at_col(z, other)]
+    for t in range(1, n_gx):
+        partners.append(at_row((gx + t) % n_gx * n_lo + lo, core))
+    for t in range(1, n_lo):
+        partners.append(at_row(gx * n_lo + (lo + t) % n_lo, core))
+
+    def greet(to):
+        pl.semaphore_signal(barrier, inc=1, device_id=to, device_id_type=MESH)
 
     word_copy = pltpu.make_async_copy(words, word_in, local_sem.at[0])
     label_copy = pltpu.make_async_copy(labels, label_in, local_sem.at[1])
     word_copy.start()
     label_copy.start()
     for p in partners:
-        pl.semaphore_signal(barrier, inc=1, device_id=p, device_id_type=MESH)
+        greet(p)
+    pl.when(up)(lambda: greet(at_col(z + 1, core)))
+    pl.when(down)(lambda: greet(at_col(z - 1, core)))
     own_rows = pl.ds(pl.multiple_of(rslot * own, own), own)
     own_cols = pl.ds(pl.multiple_of(cslot * own, own), own)
     keep = [
         pltpu.make_async_copy(samples, row_s.at[own_rows], local_sem.at[2]),
         pltpu.make_async_copy(corpus, row_c.at[own_rows], local_sem.at[3]),
         pltpu.make_async_copy(samples, col_s.at[own_cols], local_sem.at[4]),
+        pltpu.make_async_copy(grid, grid_in, local_sem.at[5]),
+        pltpu.make_async_copy(pick, pick_in, local_sem.at[6]),
     ]
     for c in keep:
         c.start()
 
-    pl.semaphore_wait(barrier, len(partners))
-
     def remote(src, dst, send, recv, to):
         return pltpu.make_async_remote_copy(
             src_ref=src, dst_ref=dst, send_sem=send, recv_sem=recv, device_id=to, device_id_type=MESH)
 
-    sends = []
-    col_in, fw_in, rs_in, rc_in = [], [], [], []
-
-    def col_block(slot):
-        return col_s.at[pl.ds(pl.multiple_of(slot * own, own), own)]
-
-    def row_block(ref, slot):
-        return ref.at[pl.ds(pl.multiple_of(slot * own, own), own)]
-
-    for t in range(1, n_hi):
-        to = (z + t) % n_hi
-        c = remote(samples, col_block(cslot), cs_send.at[t], cs_recv.at[z], at_col(to, core))
+    sends, cond_sends = [], []
+
+    def go(c):
         c.start()
         sends.append(c)
-    for t in range(1, n_row):
-        to = (rslot + t) % n_row
-        c = remote(samples, row_block(row_s, rslot), rs_send.at[t], rs_recv.at[rslot], at_row(to, core))
-        c.start()
-        sends.append(c)
-    c = remote(samples, col_block(cslot), fw_send.at[z], fw_recv.at[z], at_col(z, other))
-    c.start()
-    sends.append(c)
+
+    def go_if(cond, c):
+        pl.when(cond)(c.start)
+        cond_sends.append((cond, c))
+
+    def block(ref, slot):
+        return ref.at[pl.ds(pl.multiple_of(slot * own, own), own)]
 
     word_copy.wait()
     label_copy.wait()
@@ -122,30 +117,84 @@
     col_pack[cslot] = packed
     row_pack[rslot] = packed
 
-    for t in range(1, n_col):
-        to = (cslot + t) % n_col
-        c = remote(col_pack.at[cslot], col_pack.at[cslot], cp_send.at[t], cp_recv.at[cslot],
-                   at_col(to // CORES, to % CORES))
-        c.start()
-        sends.append(c)
-    for t in range(1, n_row):
-        to = (rslot + t) % n_row
-        c = remote(row_pack.at[rslot], row_pack.at[rslot], rp_send.at[t], rp_recv.at[rslot], at_row(to, core))
-        c.start()
-        sends.append(c)
-    for t in range(1, n_row):
-        to = (rslot + t) % n_row
-        c = remote(corpus, row_block(row_c, rslot), rc_send.at[t], rc_recv.at[rslot], at_row(to, core))
-        c.start()
-        sends.append(c)
-
-    for t in range(1, n_hi):
-        src = (z + n_hi - t) % n_hi
-        block = col_block(src * CORES + core)
-        remote(samples, block, cs_send.at[t], cs_recv.at[src], at_col(src, core)).wait_recv()
-        c = remote(block, block, fw_send.at[src], fw_recv.at[src], at_col(z, other))
-        c.start()
-        sends.append(c)
+    pl.semaphore_wait(barrier, len(partners) + up.astype(jnp.int32) + down.astype(jnp.int32))
+
+    def hop(tile, src, step, to_z, way):
+        if tile:
+            ref = col_pack.at[src * CORES + core]
+            return remote(ref, ref, cp_send.at[way, step], cp_recv.at[src], at_col(to_z, core))
+        ref = block(col_s, src * CORES + core)
+        return remote(samples if step == 0 else ref, ref, cs_send.at[way, step], cs_recv.at[src], at_col(to_z, core))
+
+    def side(tile, src):
+        if tile:
+            ref = col_pack.at[src * CORES + core]
+            return remote(ref, ref, fp_send.at[src], fp_recv.at[src], at_col(z, other))
+        ref = block(col_s, src * CORES + core)
+        return remote(ref, ref, fw_send.at[src], fw_recv.at[src], at_col(z, other))
+
+    def row_hop(which, slot, to, mine=False):
+        ref, send, recv = {"p": (row_pack, rp_send, rp_recv), "s": (row_s, rs_send, rs_recv),
+                           "c": (row_c, rc_send, rc_recv)}[which]
+        if which == "p":
+            dst = ref.at[slot]
+            src = dst
+        else:
+            dst = block(ref, slot)
+            src = {"s": samples, "c": corpus}[which] if mine else dst
+        return remote(src, dst, send.at[slot, to], recv.at[slot], at_row(to, core))
+
+    def xs(slot):
+        return [(slot // n_lo + t) % n_gx * n_lo + slot % n_lo for t in range(1, n_gx)]
+
+    def ys(slot):
+        return [slot // n_lo * n_lo + (slot % n_lo + t) % n_lo for t in range(1, n_lo)]
+
+    for tile in (True, False):
+        go_if(down, hop(tile, z, 0, z - 1, 0))
+        go_if(up, hop(tile, z, 0, z + 1, 1))
+        for which in ("p",) if tile else ("s", "c"):
+            for to in xs(rslot) + ys(rslot):
+                go(row_hop(which, rslot, to, mine=True))
+        if tile:
+            go(side(True, z))
+    go(remote(samples, block(col_s, cslot), fw_send.at[z], fw_recv.at[z], at_col(z, other)))
+
+    def chain(tile, way):
+        for d in range(1, n_hi):
+            src = z - d if way == 1 else z + d
+            here = src >= 0 if way == 1 else src < n_hi
+            onward = here & (up if way == 1 else down)
+            src = jnp.clip(src, 0, n_hi - 1)
+            nxt = jnp.clip(z + 1 if way == 1 else z - 1, 0, n_hi - 1)
+            step = min(d, n_hi - 2)
+            c = hop(tile, src, step, nxt, 1 if way == 1 else 0)
+            f = side(tile, src)
+
+            @pl.when(here)
+            def _():
+                c.wait_recv()
+                f.start()
+
+            if d < n_hi - 1:
+                pl.when(onward)(c.start)
+                cond_sends.append((onward, c))
+            cond_sends.append((here, f))
+
+    def turn(which):
+        first, then = (ys, xs) if which == "c" else (xs, ys)
+        for src in first(rslot):
+            row_hop(which, src, rslot).wait_recv()
+            for to in then(rslot):
+                go(row_hop(which, src, to))
+
+    turn("p")
+    chain(True, 1)
+    turn("s")
+    turn("c")
+    chain(False, 1)
+    chain(True, 0)
+    chain(False, 0)
 
     lane = lax.broadcasted_iota(jnp.int32, (8, 128), 1)
     label_lane = lane - lane % width + n_words
@@ -172,13 +221,18 @@
                 parts.append(jnp.where((got & mask[t]) != 0, 1.0, -1.0).astype(F32))
             dst[pl.ds(base, own), pl.ds(128 * t, 128)] = jnp.concatenate(parts, axis=0).astype(dst.dtype)
 
-    for t in range(1, n_col):
-        src = (cslot + n_col - t) % n_col
-        remote(col_pack.at[src], col_pack.at[src], cp_send.at[t], cp_recv.at[src],
-               at_col(src // CORES, src % CORES)).wait_recv()
-    for t in range(1, n_row):
-        src = (rslot + n_row - t) % n_row
-        remote(row_pack.at[src], row_pack.at[src], rp_send.at[t], rp_recv.at[src], at_row(src, core)).wait_recv()
+    def late(which):
+        first, then = (ys, xs) if which == "c" else (xs, ys)
+        for src in then(rslot):
+            row_hop(which, src, rslot).wait_recv()
+            for far in first(src):
+                row_hop(which, far, rslot).wait_recv()
+
+    late("p")
+    for t in range(n_hi):
+        src = (z + t) % n_hi
+        ref = col_pack.at[src * CORES + other]
+        remote(ref, ref, fp_send.at[src], fp_recv.at[src], at_col(z, other)).wait_recv()
     for slot in range(n_col):
         expand(col_pack[slot], col_vec, slot * own)
     for slot in range(n_row):
@@ -186,19 +240,16 @@
 
     for c in keep:
         c.wait()
+    late("s")
+    late("c")
+    pl.semaphore_signal(pair_sem, inc=1, device_id=at_col(z, other), device_id_type=MESH)
     for t in range(n_hi):
-        src = (z + n_hi - t) % n_hi
-        block = col_block(src * CORES + other)
-        remote(samples, block, fw_send.at[src], fw_recv.at[src], at_col(z, other)).wait_recv()
-    for t in range(1, n_row):
-        src = (rslot + n_row - t) % n_row
-        remote(samples, row_block(row_s, src), rs_send.at[t], rs_recv.at[src], at_row(src, core)).wait_recv()
-    for t in range(1, n_row):
-        src = (rslot + n_row - t) % n_row
-        remote(corpus, row_block(row_c, src), rc_send.at[t], rc_recv.at[src], at_row(src, core)).wait_recv()
+        src = (z + t) % n_hi
+        ref = block(col_s, src * CORES + other)
+        remote(ref, ref, fw_send.at[src], fw_recv.at[src], at_col(z, other)).wait_recv()
 
     rb, cb = min(128, rows), min(256, cols)
-    gains = [jnp.full((1, 1), -0.5 * LOG2E, F32) / jnp.full((1, 1), grid[pick[b]], F32) for b in range(n_bands)]
+    gains = [jnp.full((1, 1), -0.5 * LOG2E, F32) / jnp.full((1, 1), grid_in[pick_in[b]], F32) for b in range(n_bands)]
     diag = lax.broadcasted_iota(jnp.int32, (cb, cb), 0) == lax.broadcasted_iota(jnp.int32, (cb, cb), 1)
     if rows > rb or cols > cb:
         part1[pslot] = jnp.zeros(part1.shape[1:], F32)
@@ -239,6 +290,7 @@
 
     loop(cols // cb, column_chunk)
 
+    pl.semaphore_wait(pair_sem, 1)
     for t in range(1, n_plane):
         to = (pslot + t) % n_plane
         c = remote(part1.at[pslot], part1.at[pslot], p1_send.at[t], p1_recv.at[pslot],
@@ -284,6 +336,8 @@
     score_out[...] = jnp.sum(jnp.where(spot, score, 0.0), axis=0, keepdims=True)
     for c in sends:
         c.wait_send()
+    for cond, c in cond_sends:
+        pl.when(cond)(c.wait_send)
 
 
 def per_device(n_grp, n_dev, samples, labels, words, corpus, grid, pick):
@@ -293,10 +347,9 @@
     own, width = samples.shape
     rows, cols = n_row * own, n_col * own
     n_bands, n_vec = pick.shape[0], 512
-    dma = lambda n: pltpu.SemaphoreType.DMA((n,))
+    dma = lambda *n: pltpu.SemaphoreType.DMA(n)
     any_ = pl.BlockSpec(memory_space=pl.ANY)
     vmem = pl.BlockSpec(memory_space=pltpu.VMEM)
-    smem = pl.BlockSpec(memory_space=pltpu.SMEM)
     quad, score, proof = pl.pallas_call(
         functools.partial(kernel, (n_gx, n_lo, n_hi)),
         out_shape=(
@@ -304,7 +357,7 @@
             jax.ShapeDtypeStruct((1, n_bands), F32),
             jax.ShapeDtypeStruct((n_bands, own), F32),
         ),
-        in_specs=[any_, any_, any_, any_, smem, smem],
+        in_specs=[any_] * 6,
         out_specs=(vmem, vmem, vmem),
         scratch_shapes=[
             pltpu.VMEM((rows, width), BF16),
@@ -312,19 +365,22 @@
             pltpu.VMEM((cols, width), BF16),
             pltpu.VMEM(words.shape, jnp.int32),
             pltpu.VMEM((1, own), jnp.int32),
+            pltpu.SMEM(grid.shape, F32),
+            pltpu.SMEM(pick.shape, jnp.int32),
             pltpu.VMEM((n_row, 8, 128), jnp.int32),
             pltpu.VMEM((n_col, 8, 128), jnp.int32),
             pltpu.VMEM((rows, n_vec), F32),
             pltpu.VMEM((cols, n_vec), BF16),
             pltpu.VMEM((n_plane, n_bands, n_vec + rows), F32),
             pltpu.VMEM((n_hi, n_bands, n_vec), F32),
-            dma(5),
-            dma(n_row), dma(n_row), dma(n_col), dma(n_col), dma(n_row), dma(n_row),
-            dma(n_row), dma(n_row), dma(n_hi), dma(n_hi), dma(n_hi), dma(n_hi),
+            pltpu.SemaphoreType.REGULAR,
+            dma(7),
+            dma(n_row, n_row), dma(n_row), dma(n_row, n_row), dma(n_row), dma(n_row, n_row), dma(n_row),
+            dma(2, n_hi), dma(n_hi), dma(2, n_hi), dma(n_hi), dma(n_hi), dma(n_hi), dma(n_hi), dma(n_hi),
             dma(n_plane), dma(n_plane), dma(n_hi), dma(n_hi),
         ],
         compiler_params=pltpu.CompilerParams(
-            collective_id=0, has_side_effects=True, vmem_limit_bytes=48 * 1024 * 1024),
+            collective_id=0, has_side_effects=True, vmem_limit_bytes=62 * 1024 * 1024),
         name="two_sample",
     )(samples, labels.reshape(1, own), words, corpus, grid, pick)
     return quad, score.reshape(n_bands), proof

time: 30.9 us -> 31.6 us (1.023)
  Pallas kernels: 25.2 us -> 28.3 us
  local copies, waits for them, and re-layouts: 4.75 us -> 2.39 us
    pallas_call x1, Pallas kernels: 25.2 us -> 28.3 us  [per_device(): pl.pallas_call(functools.partial(kernel, (n_gx, n_lo, n_hi)), out_shape=(...]
    unnamed x15 -> x7, local copies, waits for them, and re-layouts: 4.75 us -> 2.39 us
where the time goes in v2:
time: 31.6 us; the launch traced here: 31.4 us
  Pallas kernels  28.3 us (90%)
  local copies, waits for them, and re-layouts  2.39 us (8%)
  between operations  0.66 us (2%)
    pallas_call x1, Pallas kernels, per_device(): pl.pallas_call(functools.partial(kernel, (n_gx, n_lo, n_hi)), out_shape=(...  28.3 us
    unnamed x7, local copies, waits for them, and re-layouts  2.39 us

profile of v2, /device:TPU:0, one launch (start us, length us, event | category | flops | bytes accessed | tf_op | source)
XLA Modules:
  0.0 31.4 jit_solution(10029992479888890119)
XLA Ops:
  0.6 28.3 %two_sample.1 = (f32[4,512]{1,0:T(4,128)}, f32[1,4]{1,0:T(1,128)}, f32[4,32]{1,0:T(4,128)}) custom-call(bf16[32,1024]{1,0:T(8,128)(2,1)} %samples.1, s32[1,32]{1,0:T(1,128)} %bitcast.2, s32[32,25]{1,0:T(8,128)} %words.1, bf16[32,1024]{1,0:T(8,128)(2,1)} %corpus.1, f32[16]{0:T(128)} %grid.1, s32[4]{0:T(128)} %pick.1), custom_call_target="tpu_custom_call" | custom-call | tf_op jit(solution)/shard_map/two_sample/pallas_call | solution.py:353
  29.0 0.0 copy-start.1
  29.0 0.0 copy-start
  29.0 1.3 %copy.12 = f32[4,512]{1,0:T(4,128)} copy(f32[4,512]{1,0:T(4,128)} %get-tuple-element.12) | data formatting | bytes 16384
  30.3 0.0 copy-done.1
  30.3 0.5 %copy.13 = f32[4]{0:T(128)} copy(f32[4]{0:T(128)S(1)} %bitcast.3) | data formatting | bytes 32
  30.8 0.0 copy-done
  30.8 0.6 %copy.14 = f32[4,32]{1,0:T(4,128)} copy(f32[4,32]{1,0:T(4,128)S(1)} %copy-done) | data formatting | bytes 1024
Async XLA Ops:
  29.0 1.3 %copy-start.1 = (f32[1,4]{1,0:T(1,128)S(1)}, f32[1,4]{1,0:T(1,128)}, u32[]{:S(2)}) copy-start(f32[1,4]{1,0:T(1,128)} %get-tuple-element.7) | copy-start | bytes 52
  29.0 1.8 %copy-start = (f32[4,32]{1,0:T(4,128)S(1)}, f32[4,32]{1,0:T(4,128)}, u32[]{:S(2)}) copy-start(f32[4,32]{1,0:T(4,128)} %get-tuple-element.14) | copy-start | bytes 1540

commit v3 on v1

--- a/solution.py
+++ b/solution.py
@@ -28,7 +28,7 @@
 
 
 def kernel(geo, samples, labels, words, corpus, grid, pick, quad_out, score_out, proof_out,
-           row_s, row_c, col_s, word_in, label_in, row_pack, col_pack, row_vec, col_vec,
+           row_s, row_c, col_s, word_in, label_in, grid_in, pick_in, row_pack, col_pack, row_vec, col_vec,
            part1, part2, local_sem, rp_send, rp_recv, cp_send, cp_recv, rs_send, rs_recv,
            rc_send, rc_recv, cs_send, cs_recv, fw_send, fw_recv, p1_send, p1_recv, p2_send, p2_recv):
     n_gx, n_lo, n_hi = geo
@@ -74,38 +74,12 @@
         pltpu.make_async_copy(samples, row_s.at[own_rows], local_sem.at[2]),
         pltpu.make_async_copy(corpus, row_c.at[own_rows], local_sem.at[3]),
         pltpu.make_async_copy(samples, col_s.at[own_cols], local_sem.at[4]),
+        pltpu.make_async_copy(grid, grid_in, local_sem.at[5]),
+        pltpu.make_async_copy(pick, pick_in, local_sem.at[6]),
     ]
     for c in keep:
         c.start()
 
-    pl.semaphore_wait(barrier, len(partners))
-
-    def remote(src, dst, send, recv, to):
-        return pltpu.make_async_remote_copy(
-            src_ref=src, dst_ref=dst, send_sem=send, recv_sem=recv, device_id=to, device_id_type=MESH)
-
-    sends = []
-    col_in, fw_in, rs_in, rc_in = [], [], [], []
-
-    def col_block(slot):
-        return col_s.at[pl.ds(pl.multiple_of(slot * own, own), own)]
-
-    def row_block(ref, slot):
-        return ref.at[pl.ds(pl.multiple_of(slot * own, own), own)]
-
-    for t in range(1, n_hi):
-        to = (z + t) % n_hi
-        c = remote(samples, col_block(cslot), cs_send.at[t], cs_recv.at[z], at_col(to, core))
-        c.start()
-        sends.append(c)
-    for t in range(1, n_row):
-        to = (rslot + t) % n_row
-        c = remote(samples, row_block(row_s, rslot), rs_send.at[t], rs_recv.at[rslot], at_row(to, core))
-        c.start()
-        sends.append(c)
-    c = remote(samples, col_block(cslot), fw_send.at[z], fw_recv.at[z], at_col(z, other))
-    c.start()
-    sends.append(c)
 
     word_copy.wait()
     label_copy.wait()
@@ -122,6 +96,21 @@
     col_pack[cslot] = packed
     row_pack[rslot] = packed
 
+    pl.semaphore_wait(barrier, len(partners))
+
+    def remote(src, dst, send, recv, to):
+        return pltpu.make_async_remote_copy(
+            src_ref=src, dst_ref=dst, send_sem=send, recv_sem=recv, device_id=to, device_id_type=MESH)
+
+    sends = []
+    col_in, fw_in, rs_in, rc_in = [], [], [], []
+
+    def col_block(slot):
+        return col_s.at[pl.ds(pl.multiple_of(slot * own, own), own)]
+
+    def row_block(ref, slot):
+        return ref.at[pl.ds(pl.multiple_of(slot * own, own), own)]
+
     for t in range(1, n_col):
         to = (cslot + t) % n_col
         c = remote(col_pack.at[cslot], col_pack.at[cslot], cp_send.at[t], cp_recv.at[cslot],
@@ -133,6 +122,20 @@
         c = remote(row_pack.at[rslot], row_pack.at[rslot], rp_send.at[t], rp_recv.at[rslot], at_row(to, core))
         c.start()
         sends.append(c)
+    for t in range(1, n_hi):
+        to = (z + t) % n_hi
+        c = remote(samples, col_block(cslot), cs_send.at[t], cs_recv.at[z], at_col(to, core))
+        c.start()
+        sends.append(c)
+    for t in range(1, n_row):
+        to = (rslot + t) % n_row
+        c = remote(samples, row_block(row_s, rslot), rs_send.at[t], rs_recv.at[rslot], at_row(to, core))
+        c.start()
+        sends.append(c)
+    c = remote(samples, col_block(cslot), fw_send.at[z], fw_recv.at[z], at_col(z, other))
+    c.start()
+    sends.append(c)
+
     for t in range(1, n_row):
         to = (rslot + t) % n_row
         c = remote(corpus, row_block(row_c, rslot), rc_send.at[t], rc_recv.at[rslot], at_row(to, core))
@@ -198,7 +201,7 @@
         remote(corpus, row_block(row_c, src), rc_send.at[t], rc_recv.at[src], at_row(src, core)).wait_recv()
 
     rb, cb = min(128, rows), min(256, cols)
-    gains = [jnp.full((1, 1), -0.5 * LOG2E, F32) / jnp.full((1, 1), grid[pick[b]], F32) for b in range(n_bands)]
+    gains = [jnp.full((1, 1), -0.5 * LOG2E, F32) / jnp.full((1, 1), grid_in[pick_in[b]], F32) for b in range(n_bands)]
     diag = lax.broadcasted_iota(jnp.int32, (cb, cb), 0) == lax.broadcasted_iota(jnp.int32, (cb, cb), 1)
     if rows > rb or cols > cb:
         part1[pslot] = jnp.zeros(part1.shape[1:], F32)
@@ -296,7 +299,6 @@
     dma = lambda n: pltpu.SemaphoreType.DMA((n,))
     any_ = pl.BlockSpec(memory_space=pl.ANY)
     vmem = pl.BlockSpec(memory_space=pltpu.VMEM)
-    smem = pl.BlockSpec(memory_space=pltpu.SMEM)
     quad, score, proof = pl.pallas_call(
         functools.partial(kernel, (n_gx, n_lo, n_hi)),
         out_shape=(
@@ -304,7 +306,7 @@
             jax.ShapeDtypeStruct((1, n_bands), F32),
             jax.ShapeDtypeStruct((n_bands, own), F32),
         ),
-        in_specs=[any_, any_, any_, any_, smem, smem],
+        in_specs=[any_] * 6,
         out_specs=(vmem, vmem, vmem),
         scratch_shapes=[
             pltpu.VMEM((rows, width), BF16),
@@ -312,19 +314,21 @@
             pltpu.VMEM((cols, width), BF16),
             pltpu.VMEM(words.shape, jnp.int32),
             pltpu.VMEM((1, own), jnp.int32),
+            pltpu.SMEM(grid.shape, F32),
+            pltpu.SMEM(pick.shape, jnp.int32),
             pltpu.VMEM((n_row, 8, 128), jnp.int32),
             pltpu.VMEM((n_col, 8, 128), jnp.int32),
             pltpu.VMEM((rows, n_vec), F32),
             pltpu.VMEM((cols, n_vec), BF16),
             pltpu.VMEM((n_plane, n_bands, n_vec + rows), F32),
             pltpu.VMEM((n_hi, n_bands, n_vec), F32),
-            dma(5),
+            dma(7),
             dma(n_row), dma(n_row), dma(n_col), dma(n_col), dma(n_row), dma(n_row),
             dma(n_row), dma(n_row), dma(n_hi), dma(n_hi), dma(n_hi), dma(n_hi),
             dma(n_plane), dma(n_plane), dma(n_hi), dma(n_hi),
         ],
         compiler_params=pltpu.CompilerParams(
-            collective_id=0, has_side_effects=True, vmem_limit_bytes=48 * 1024 * 1024),
+            collective_id=0, has_side_effects=True, vmem_limit_bytes=62 * 1024 * 1024),
         name="two_sample",
     )(samples, labels.reshape(1, own), words, corpus, grid, pick)
     return quad, score.reshape(n_bands), proof

time: 30.9 us -> 28.7 us (0.929)
  local copies, waits for them, and re-layouts: 4.75 us -> 2.39 us
    unnamed x15 -> x7, local copies, waits for them, and re-layouts: 4.75 us -> 2.39 us
where the time goes in v3:
time: 28.7 us; the launch traced here: 28.5 us
  Pallas kernels  25.4 us (89%)
  local copies, waits for them, and re-layouts  2.39 us (8%)
  between operations  0.66 us (2%)
    pallas_call x1, Pallas kernels, per_device(): pl.pallas_call(functools.partial(kernel, (n_gx, n_lo, n_hi)), out_shape=(...  25.4 us
    unnamed x7, local copies, waits for them, and re-layouts  2.39 us

profile of v3, /device:TPU:0, one launch (start us, length us, event | category | flops | bytes accessed | tf_op | source)
XLA Modules:
  0.0 28.5 jit_solution(18380093260030432514)
XLA Ops:
  0.6 25.4 %two_sample.1 = (f32[4,512]{1,0:T(4,128)}, f32[1,4]{1,0:T(1,128)}, f32[4,32]{1,0:T(4,128)}) custom-call(bf16[32,1024]{1,0:T(8,128)(2,1)} %samples.1, s32[1,32]{1,0:T(1,128)} %bitcast.2, s32[32,25]{1,0:T(8,128)} %words.1, bf16[32,1024]{1,0:T(8,128)(2,1)} %corpus.1, f32[16]{0:T(128)} %grid.1, s32[4]{0:T(128)} %pick.1), custom_call_target="tpu_custom_call" | custom-call | tf_op jit(solution)/shard_map/two_sample/pallas_call | solution.py:302
  26.1 0.0 copy-start.1
  26.1 0.0 copy-start
  26.1 1.3 %copy.12 = f32[4,512]{1,0:T(4,128)} copy(f32[4,512]{1,0:T(4,128)} %get-tuple-element.12) | data formatting | bytes 16384
  27.4 0.0 copy-done.1
  27.4 0.5 %copy.13 = f32[4]{0:T(128)} copy(f32[4]{0:T(128)S(1)} %bitcast.3) | data formatting | bytes 32
  27.9 0.0 copy-done
  27.9 0.6 %copy.14 = f32[4,32]{1,0:T(4,128)} copy(f32[4,32]{1,0:T(4,128)S(1)} %copy-done) | data formatting | bytes 1024
Async XLA Ops:
  26.1 1.3 %copy-start.1 = (f32[1,4]{1,0:T(1,128)S(1)}, f32[1,4]{1,0:T(1,128)}, u32[]{:S(2)}) copy-start(f32[1,4]{1,0:T(1,128)} %get-tuple-element.7) | copy-start | bytes 52
  26.1 1.8 %copy-start = (f32[4,32]{1,0:T(4,128)S(1)}, f32[4,32]{1,0:T(4,128)}, u32[]{:S(2)}) copy-start(f32[4,32]{1,0:T(4,128)} %get-tuple-element.14) | copy-start | bytes 1540

commit v4 on v3

--- a/solution.py
+++ b/solution.py
@@ -27,7 +27,7 @@
     return index * size if isinstance(index, int) else pl.multiple_of(index * size, size)
 
 
-def kernel(geo, samples, labels, words, corpus, grid, pick, quad_out, score_out, proof_out,
+def kernel(geo, samples, labels, words, corpus, grid, pick, quad_out, proof_out,
            row_s, row_c, col_s, word_in, label_in, grid_in, pick_in, row_pack, col_pack, row_vec, col_vec,
            part1, part2, local_sem, rp_send, rp_recv, cp_send, cp_recv, rs_send, rs_recv,
            rc_send, rc_recv, cs_send, cs_recv, fw_send, fw_recv, p1_send, p1_recv, p2_send, p2_recv):
@@ -276,6 +276,15 @@
         quad = quad + part2[slot]
     quad = quad * F32(1.0 / total)
     quad_out[...] = quad
+    for c in sends:
+        c.wait_send()
+
+
+def finish(quad_in, proof_in, quad_out, score_out, proof_out):
+    quad = quad_in[...]
+    quad_out[...] = quad
+    proof_out[...] = proof_in[...]
+    n_bands, n_vec = quad.shape
     boot = lax.broadcasted_iota(jnp.int32, quad.shape, 1) > 0
     count = F32(1.0 / (n_vec - 1))
     centre = jnp.sum(jnp.where(boot, quad, 0.0), axis=1, keepdims=True) * count
@@ -285,8 +294,6 @@
     spot = lax.broadcasted_iota(jnp.int32, (n_bands, n_bands), 0) == lax.broadcasted_iota(
         jnp.int32, (n_bands, n_bands), 1)
     score_out[...] = jnp.sum(jnp.where(spot, score, 0.0), axis=0, keepdims=True)
-    for c in sends:
-        c.wait_send()
 
 
 def per_device(n_grp, n_dev, samples, labels, words, corpus, grid, pick):
@@ -299,15 +306,14 @@
     dma = lambda n: pltpu.SemaphoreType.DMA((n,))
     any_ = pl.BlockSpec(memory_space=pl.ANY)
     vmem = pl.BlockSpec(memory_space=pltpu.VMEM)
-    quad, score, proof = pl.pallas_call(
+    quad, proof = pl.pallas_call(
         functools.partial(kernel, (n_gx, n_lo, n_hi)),
         out_shape=(
             jax.ShapeDtypeStruct((n_bands, n_vec), F32),
-            jax.ShapeDtypeStruct((1, n_bands), F32),
             jax.ShapeDtypeStruct((n_bands, own), F32),
         ),
         in_specs=[any_] * 6,
-        out_specs=(vmem, vmem, vmem),
+        out_specs=(vmem, vmem),
         scratch_shapes=[
             pltpu.VMEM((rows, width), BF16),
             pltpu.VMEM((rows, width), BF16),
@@ -331,6 +337,17 @@
             collective_id=0, has_side_effects=True, vmem_limit_bytes=62 * 1024 * 1024),
         name="two_sample",
     )(samples, labels.reshape(1, own), words, corpus, grid, pick)
+    quad, score, proof = pl.pallas_call(
+        finish,
+        out_shape=(
+            jax.ShapeDtypeStruct((n_bands, n_vec), F32),
+            jax.ShapeDtypeStruct((1, n_bands), F32),
+            jax.ShapeDtypeStruct((n_bands, own), F32),
+        ),
+        in_specs=[vmem, vmem],
+        out_specs=(vmem, vmem, vmem),
+        name="finish",
+    )(quad, proof)
     return quad, score.reshape(n_bands), proof
 
 

time: 28.7 us -> 27.7 us (0.965)
  local copies, waits for them, and re-layouts: 2.39 us -> 0 us
  Pallas kernels: 25.4 us -> 26.7 us
    unnamed x7 -> x0, local copies, waits for them, and re-layouts: 2.39 us -> none
    pallas_call x0 -> x1, Pallas kernels: none -> 1.55 us  [per_device(): pl.pallas_call(finish, out_shape=(jax.ShapeDtypeStruct((n_bands, n_vec),...]
where the time goes in v4:
time: 27.7 us; the launch traced here: 27.4 us
  Pallas kernels  26.7 us (96%)
  between operations  0.64 us (2%)
    pallas_call x1, Pallas kernels, per_device(): pl.pallas_call(functools.partial(kernel, (n_gx, n_lo, n_hi)), out_shape=(...  25.2 us
    pallas_call x1, Pallas kernels, per_device(): pl.pallas_call(finish, out_shape=(jax.ShapeDtypeStruct((n_bands, n_vec),...  1.55 us

profile of v4, /device:TPU:0, one launch (start us, length us, event | category | flops | bytes accessed | tf_op | source)
XLA Modules:
  0.0 27.4 jit_solution(12304038123851032460)
XLA Ops:
  0.6 25.2 %two_sample.1 = (f32[4,512]{1,0:T(4,128)}, f32[4,32]{1,0:T(4,128)}) custom-call(bf16[32,1024]{1,0:T(8,128)(2,1)} %samples.1, s32[1,32]{1,0:T(1,128)} %bitcast.2, s32[32,25]{1,0:T(8,128)} %words.1, bf16[32,1024]{1,0:T(8,128)(2,1)} %corpus.1, f32[16]{0:T(128)} %grid.1, s32[4]{0:T(128)} %pick.1), custom_call_target="tpu_custom_call" | custom-call | tf_op jit(solution)/shard_map/two_sample/pallas_call | solution.py:309
  25.8 1.6 %finish.1 = (f32[4,512]{1,0:T(4,128)}, f32[1,4]{1,0:T(1,128)}, f32[4,32]{1,0:T(4,128)}) custom-call(f32[4,512]{1,0:T(4,128)} %get-tuple-element.8.quad_in, f32[4,32]{1,0:T(4,128)} %get-tuple-element.9.proof_in), custom_call_target="tpu_custom_call" | custom-call | tf_op jit(solution)/shard_map/finish/pallas_call | solution.py:340

commit v5 on v4

--- a/solution.py
+++ b/solution.py
@@ -29,8 +29,8 @@
 
 def kernel(geo, samples, labels, words, corpus, grid, pick, quad_out, proof_out,
            row_s, row_c, col_s, word_in, label_in, grid_in, pick_in, row_pack, col_pack, row_vec, col_vec,
-           part1, part2, local_sem, rp_send, rp_recv, cp_send, cp_recv, rs_send, rs_recv,
-           rc_send, rc_recv, cs_send, cs_recv, fw_send, fw_recv, p1_send, p1_recv, p2_send, p2_recv):
+           part1, part2, part3, local_sem, rp_send, rp_recv, cp_send, cp_recv, rs_send, rs_recv,
+           rc_send, rc_recv, cs_send, cs_recv, fw_send, fw_recv, p1_send, p1_recv, p2_send, p2_recv, p3_send, p3_recv):
     n_gx, n_lo, n_hi = geo
     own = samples.shape[0]
     n_bands, n_vec = quad_out.shape
@@ -196,15 +196,13 @@
     for t in range(1, n_row):
         src = (rslot + n_row - t) % n_row
         remote(samples, row_block(row_s, src), rs_send.at[t], rs_recv.at[src], at_row(src, core)).wait_recv()
-    for t in range(1, n_row):
-        src = (rslot + n_row - t) % n_row
-        remote(corpus, row_block(row_c, src), rc_send.at[t], rc_recv.at[src], at_row(src, core)).wait_recv()
 
     rb, cb = min(128, rows), min(256, cols)
     gains = [jnp.full((1, 1), -0.5 * LOG2E, F32) / jnp.full((1, 1), grid_in[pick_in[b]], F32) for b in range(n_bands)]
     diag = lax.broadcasted_iota(jnp.int32, (cb, cb), 0) == lax.broadcasted_iota(jnp.int32, (cb, cb), 1)
     if rows > rb or cols > cb:
         part1[pslot] = jnp.zeros(part1.shape[1:], F32)
+        part3[rslot] = jnp.zeros(part3.shape[1:], F32)
 
     def squares(x):
         wide = x.astype(F32)
@@ -215,15 +213,18 @@
         dist = squares(left) + right_sq - 2.0 * cross
         return jnp.concatenate([jnp.exp2(dist * g).astype(BF16) for g in gains], axis=0)
 
-    def add_to(lanes, value):
+    def add_to(ref, slot, lanes, value):
         if rows > rb or cols > cb:
-            value = part1[pslot, :, lanes] + value
-        part1[pslot, :, lanes] = value
-
-    def column_chunk(cc):
+            value = ref[slot, :, lanes] + value
+        ref[slot, :, lanes] = value
+
+    def columns(cc):
         here = pl.ds(aligned(cc, cb), cb)
         right = col_s[here, :]
-        right_sq = jnp.sum(jnp.where(diag, squares(right), 0.0), axis=0, keepdims=True)
+        return here, right, jnp.sum(jnp.where(diag, squares(right), 0.0), axis=0, keepdims=True)
+
+    def test_chunk(cc):
+        here, right, right_sq = columns(cc)
         vec = col_vec[here, :]
 
         def row_chunk(rc):
@@ -232,15 +233,24 @@
             prod = jnp.dot(kern, vec, preferred_element_type=F32)
             mine = row_vec[there, :]
             forms = [jnp.sum(mine * prod[b * rb:(b + 1) * rb], axis=0, keepdims=True) for b in range(n_bands)]
-            add_to(pl.ds(0, n_vec), jnp.concatenate(forms, axis=0))
+            add_to(part1, pslot, pl.ds(0, n_vec), jnp.concatenate(forms, axis=0))
+
+        loop(rows // rb, row_chunk)
+
+    def proof_chunk(cc):
+        here, right, right_sq = columns(cc)
+        vec = col_vec[here, :128]
+
+        def row_chunk(rc):
+            there = pl.ds(aligned(rc, rb), rb)
             kern = kerns(row_c[there, :], right, right_sq)
-            flat = lax.dot_general(vec[:, :128], kern, (((0,), (1,)), ((), ())), preferred_element_type=F32)
+            flat = lax.dot_general(vec, kern, (((0,), (1,)), ((), ())), preferred_element_type=F32)
             proof = jnp.concatenate([flat[0:1, b * rb:(b + 1) * rb] for b in range(n_bands)], axis=0)
-            add_to(pl.ds(aligned(rc, rb) + n_vec, rb), proof)
+            add_to(part3, rslot, there, proof)
 
         loop(rows // rb, row_chunk)
 
-    loop(cols // cb, column_chunk)
+    loop(cols // cb, test_chunk)
 
     for t in range(1, n_plane):
         to = (pslot + t) % n_plane
@@ -248,22 +258,34 @@
                    at_row(to // CORES, to % CORES))
         c.start()
         sends.append(c)
+    for t in range(1, n_row):
+        src = (rslot + n_row - t) % n_row
+        remote(corpus, row_block(row_c, src), rc_send.at[t], rc_recv.at[src], at_row(src, core)).wait_recv()
+    loop(cols // cb, proof_chunk)
+    for t in range(1, n_row):
+        to = (rslot + t) % n_row
+        c = remote(part3.at[rslot], part3.at[rslot], p3_send.at[t], p3_recv.at[rslot], at_row(to, core))
+        c.start()
+        sends.append(c)
     for t in range(1, n_plane):
         src = (pslot + n_plane - t) % n_plane
         remote(part1.at[src], part1.at[src], p1_send.at[t], p1_recv.at[src],
                at_row(src // CORES, src % CORES)).wait_recv()
-    quad = part1[0, :, :n_vec]
+    quad = part1[0]
     for slot in range(1, n_plane):
-        quad = quad + part1[slot, :, :n_vec]
+        quad = quad + part1[slot]
     part2[z] = quad
     for t in range(1, n_hi):
         to = (z + t) % n_hi
         c = remote(part2.at[z], part2.at[z], p2_send.at[t], p2_recv.at[z], at_col(to, core))
         c.start()
         sends.append(c)
-    proof = part1[core, :, n_vec:]
+    for t in range(1, n_row):
+        src = (rslot + n_row - t) % n_row
+        remote(part3.at[src], part3.at[src], p3_send.at[t], p3_recv.at[src], at_row(src, core)).wait_recv()
+    proof = part3[0]
     for slot in range(1, n_row):
-        proof = proof + part1[slot * CORES + core, :, n_vec:]
+        proof = proof + part3[slot]
     mine = jnp.zeros((n_bands, own), F32)
     for slot in range(n_row):
         mine = jnp.where(rslot == slot, proof[:, slot * own:(slot + 1) * own], mine)
@@ -326,12 +348,13 @@
             pltpu.VMEM((n_col, 8, 128), jnp.int32),
             pltpu.VMEM((rows, n_vec), F32),
             pltpu.VMEM((cols, n_vec), BF16),
-            pltpu.VMEM((n_plane, n_bands, n_vec + rows), F32),
+            pltpu.VMEM((n_plane, n_bands, n_vec), F32),
             pltpu.VMEM((n_hi, n_bands, n_vec), F32),
+            pltpu.VMEM((n_row, n_bands, rows), F32),
             dma(7),
             dma(n_row), dma(n_row), dma(n_col), dma(n_col), dma(n_row), dma(n_row),
             dma(n_row), dma(n_row), dma(n_hi), dma(n_hi), dma(n_hi), dma(n_hi),
-            dma(n_plane), dma(n_plane), dma(n_hi), dma(n_hi),
+            dma(n_plane), dma(n_plane), dma(n_hi), dma(n_hi), dma(n_row), dma(n_row),
         ],
         compiler_params=pltpu.CompilerParams(
             collective_id=0, has_side_effects=True, vmem_limit_bytes=62 * 1024 * 1024),

time: 27.7 us -> 27.2 us (0.982)
  Pallas kernels: 26.7 us -> 26.2 us
    pallas_call x1, Pallas kernels: 25.2 us -> 24.7 us  [per_device(): pl.pallas_call(functools.partial(kernel, (n_gx, n_lo, n_hi)), out_shape=(...]
where the time goes in v5:
time: 27.2 us; the launch traced here: 26.9 us
  Pallas kernels  26.2 us (96%)
  between operations  0.64 us (2%)
    pallas_call x1, Pallas kernels, per_device(): pl.pallas_call(functools.partial(kernel, (n_gx, n_lo, n_hi)), out_shape=(...  24.7 us
    pallas_call x1, Pallas kernels, per_device(): pl.pallas_call(finish, out_shape=(jax.ShapeDtypeStruct((n_bands, n_vec),...  1.55 us

profile of v5, /device:TPU:0, one launch (start us, length us, event | category | flops | bytes accessed | tf_op | source)
XLA Modules:
  0.0 26.9 jit_solution(11177320628171958819)
XLA Ops:
  0.6 24.7 %two_sample.1 = (f32[4,512]{1,0:T(4,128)}, f32[4,32]{1,0:T(4,128)}) custom-call(bf16[32,1024]{1,0:T(8,128)(2,1)} %samples.1, s32[1,32]{1,0:T(1,128)} %bitcast.2, s32[32,25]{1,0:T(8,128)} %words.1, bf16[32,1024]{1,0:T(8,128)(2,1)} %corpus.1, f32[16]{0:T(128)} %grid.1, s32[4]{0:T(128)} %pick.1), custom_call_target="tpu_custom_call" | custom-call | tf_op jit(solution)/shard_map/two_sample/pallas_call | solution.py:331
  25.3 1.6 %finish.1 = (f32[4,512]{1,0:T(4,128)}, f32[1,4]{1,0:T(1,128)}, f32[4,32]{1,0:T(4,128)}) custom-call(f32[4,512]{1,0:T(4,128)} %get-tuple-element.8.quad_in, f32[4,32]{1,0:T(4,128)} %get-tuple-element.9.proof_in), custom_call_target="tpu_custom_call" | custom-call | tf_op jit(solution)/shard_map/finish/pallas_call | solution.py:363
